TPU v7x, 128 devices: a whole 4x4x4 slice. The times are simulated.
128 devices in a mesh: grp: 4 (over z_hi, core), sub: 32 (over x, z_lo, y).
Axes of the slice: x: 4, y: 4, z: 4 (z_hi: 2, z_lo: 2; z = z_hi * 2 + z_lo), core: 2. Of those that a mesh axis runs over, the one named last changes fastest.
Arguments:
- left: bfloat16 [24576, 1536], P('sub', 'grp'), may hold values from -6 to 6
- right: bfloat16 [1536, 24576], P('sub', 'grp'), may hold values from -0.15625 to 0.15625
Outputs:
- product: bfloat16 [24576, 24576], P('sub', 'grp')
All inputs are finite; a program needn't handle non-finite values.
Results may differ from a plain program's by a relative error of at most 0.001.
Values may be sent and summed in bfloat16 or wider, within the bound.
A program may use at most 128 MiB of HBM per device.

v0:
```python
import jax
import jax.numpy as jnp
from jax import lax
from jax.sharding import PartitionSpec as P


def shards(left, right):
    left_full = lax.all_gather(left, "grp", axis=1, tiled=True)
    right_full = lax.all_gather(right, "sub", axis=0, tiled=True)
    result = jnp.dot(left_full, right_full, preferred_element_type=jnp.float32).astype(jnp.bfloat16)
    return result


def solution(mesh):
    placed = (P("sub", "grp"), P("sub", "grp"))
    return jax.shard_map(
        shards, mesh=mesh, in_specs=placed, out_specs=P("sub", "grp"), check_vma=False
    )
```

profile of v0, /device:TPU:0, one launch (start us, length us, event | category | flops | bytes accessed | tf_op | source)
XLA Modules:
  0.0 280.1 jit_solution(2022903615321726378)
XLA Ops:
  6.5 0.0 all-gather.3.cloned.1.call-start
  6.5 0.7 all-gather.3.cloned.1.call-update
  7.3 0.0 all-gather.5.cloned.1.call-start
  7.3 0.7 all-gather.5.cloned.1.call-update
  8.0 31.8 %all-gather.3.cloned.1.call-done = bf16[768,1536]{1,0:T(8,128)(2,1)} async-done(((bf16[768,384]{1,0:T(8,128)(2,1)}), bf16[768,1536]{1,0:T(8,128)(2,1)}) %all-gather.3.cloned.1.call-update) | async-done | bytes 2359312 | tf_op jit(solution)/shard_map/all_gather | solution.py:8
  39.8 213.3 %all-gather.5.cloned.1.call-done = bf16[1536,6144]{1,0:T(8,128)(2,1)} async-done(((bf16[48,6144]{1,0:T(8,128)(2,1)}), bf16[1536,6144]{1,0:T(8,128)(2,1)}) %all-gather.5.cloned.1.call-update) | async-done | bytes 18874384 | tf_op jit(solution)/shard_map/all_gather | solution.py:9
  253.0 20.3 %convolution_convert_fusion = bf16[768,6144]{1,0:T(8,128)(2,1)} fusion(bf16[768,1536]{1,0:T(8,128)(2,1)} %all-gather.3.cloned.1.call-done, bf16[1536,6144]{1,0:T(8,128)(2,1)} %all-gather.5.cloned.1.call-done), kind=kOutput, calls=%fused_computation | convolution fusion | flops 14500233216 | bytes 30670848 | tf_op jit(solution)/shard_map/dot_general | solution.py:10
Async XLA Ops:
  6.5 33.2 %all-gather.3.cloned.1.call-start = ((), (), s32[]{:S(2)}) async-start(), calls=%async_computation | async-start | bytes 2949120 | tf_op jit(solution)/shard_map/all_gather | solution.py:8
  7.3 245.8 %all-gather.5.cloned.1.call-start = ((), (), s32[]{:S(2)}) async-start(), calls=%async_computation.1 | async-start | bytes 19464192 | tf_op jit(solution)/shard_map/all_gather | solution.py:9
Sparse Core Ops, SparseCore 0:
  9.0 30.6 all-gather.2
  41.4 211.5 all-gather.4
where the time goes:
time: 281 us; the launch traced here: 280 us
  waiting for transfers between devices  246 us (88%)
  matrix products  20.3 us (7%)
  between operations  13.4 us (5%)
    all_gather x1, waiting for transfers between devices, shards(): right_full = lax.all_gather(right, 'sub', axis=0, tiled=True)  213 us
    all_gather x1, waiting for transfers between devices, shards(): left_full = lax.all_gather(left, 'grp', axis=1, tiled=True)  31.8 us
    dot_general x1, matrix products, shards(): jnp.dot(left_full, right_full, preferred_element_type=jnp.float32)  20.3 us
  transfers between devices with their start and end apart: 2, of which 2 were waited for; matrix products, arithmetic and copies ran while one was open for 0% of the time, Pallas kernels for 0%

commit v1 on v0

v1 whole, which is shorter than its diff:
```python
import functools

import jax
import jax.numpy as jnp
from jax import lax
from jax.experimental import pallas as pl
from jax.experimental.pallas import tpu as pltpu
from jax.sharding import PartitionSpec as P

MESH = pl.DeviceIdType.MESH
M, N, K, DEPTH, KL = 768, 6144, 1536, 48, 384
W = 256
NS = 5
ND = N // W - 2 * NS
NC = NS + ND
TILE = 256
OWN, MATE = 0, 1


def kernel(left, right, out, held, rows, theirs, recv, send, lrecv, lsend, orecv, osend, local):
    grp, sub = lax.axis_index("grp"), lax.axis_index("sub")
    zh, core = grp // 2, lax.rem(grp, 2)
    x, zl, y = sub // 8, lax.rem(sub // 4, 2), lax.rem(sub, 4)

    def device(x, y, zh, zl, core):
        return (zh * 2 + core, x * 8 + zl * 4 + y)

    xr, xl, yr, yl = lax.rem(x + 1, 4), lax.rem(x + 3, 4), lax.rem(y + 1, 4), lax.rem(y + 3, 4)
    x_right, x_left = device(xr, y, zh, zl, core), device(xl, y, zh, zl, core)
    y_right, y_left = device(x, yr, zh, zl, core), device(x, yl, zh, zl, core)
    mate = device(x, y, zh, 1 - zl, core)
    cross = device(x, y, 1 - zh, 1 - zl, core)
    sibling = device(x, y, zh, zl, 1 - core)
    around = (x_right, x_left, y_right, y_left, mate, cross, sibling)

    barrier = pltpu.get_barrier_semaphore()
    for other in around:
        pl.semaphore_signal(barrier, inc=1, device_id=other, device_id_type=MESH)

    def column(i, side):
        if i < NS:
            return pl.multiple_of(side * (NS * W) + i * W, 128)
        return (NS + i) * W

    def go(src, dst, ssem, rsem, to):
        copy = pltpu.make_async_remote_copy(src, dst, ssem, rsem, device_id=to, device_id_type=MESH)
        copy.start()
        return copy

    own = []
    for i in range(NC):
        copy = pltpu.make_async_copy(right.at[:, pl.ds(column(i, zl), W)], held.at[i, x, zl, y], local.at[i])
        copy.start()
        own.append(copy)
    mine = pltpu.make_async_copy(left, rows.at[OWN, :, pl.ds(pl.multiple_of(grp * KL, 128), KL)], local.at[NC])
    mine.start()
    pl.semaphore_wait(barrier, len(around))

    sent = []
    started = {}

    for i in range(NC):
        started[i, 0] = (go(right.at[:, pl.ds(column(i, 1 - zl), W)], held.at[i, x, zl, y], send.at[i, 0], recv.at[i, 0], mate),)

    def kcols(g):
        return pl.ds(pl.multiple_of(g * KL, 128), KL)

    other = (1 - zh) * 2 + core
    lcopy = {}
    lcopy["z"] = go(left, rows.at[MATE, :, kcols(grp)], lsend.at[0], lrecv.at[0], mate)
    lcopy["c"] = go(left, rows.at[MATE, :, kcols(grp)], lsend.at[1], lrecv.at[1], cross)
    lcopy["s0"] = go(left, rows.at[OWN, :, kcols(grp)], lsend.at[2], lrecv.at[2], sibling)

    def left_mate():
        lcopy["z"].wait_recv()
        block = rows.at[MATE, :, kcols(grp)]
        lcopy["c2"] = go(block, rows.at[OWN, :, kcols(grp)], lsend.at[3], lrecv.at[3], cross)
        lcopy["s1"] = go(block, block, lsend.at[4], lrecv.at[4], sibling)
        lcopy["c"].wait_recv()
        block = rows.at[MATE, :, kcols(other)]
        lcopy["s2"] = go(block, block, lsend.at[5], lrecv.at[5], sibling)

    def left_own():
        lcopy["c2"].wait_recv()
        block = rows.at[OWN, :, kcols(other)]
        lcopy["s3"] = go(block, block, lsend.at[6], lrecv.at[6], sibling)
        lcopy["s0"].wait_recv()
        mine.wait()

    def piece(i, along, a, b, z):
        return held.at[i, a, z, b] if along == 0 else held.at[i, b, z, a]

    def stage(i, k):
        first = i % 2
        if k in (1, 2):
            along = first
        else:
            along = 1 - first
        here, lo, hi = ((x, xl, xr), (y, yl, yr))[along]
        fixed = (y, x)[along] if k in (1, 2) else slice(None)
        right_to, left_to = ((x_right, x_left), (y_right, y_left))[along]
        for copy in started[i, k - 1]:
            copy.wait_recv()
        if k == 1:
            own[i].wait()
        if k in (1, 3):
            up = down = piece(i, along, here, fixed, slice(None))
        else:
            up, down = piece(i, along, lo, fixed, 0), piece(i, along, hi, fixed, 1)
        s, r = send.at[i], recv.at[i]
        started[i, k] = (
            go(up, up, s.at[2 * k - 1], r.at[2 * k - 1], right_to),
            go(down, down, s.at[2 * k], r.at[2 * k], left_to),
        )

    def multiply(side, i, write):
        block = held.at[i]

        @pl.loop(0, M // TILE)
        def _(t):
            at = pl.ds(pl.multiple_of(t * TILE, TILE), TILE)
            value = jnp.dot(rows[side, at, :], block[...].reshape(K, W), preferred_element_type=jnp.float32)
            write(at, value.astype(jnp.bfloat16))

    outs = []

    def compute_mate(i):
        def write(at, value):
            theirs[i, at, :] = value

        multiply(MATE, i, write)
        c = column(i, zl)
        outs.append(go(theirs.at[i], out.at[:, pl.ds(c, W)], osend.at[i], orecv.at[i], mate))

    def compute_own(i):
        c = column(i, zl)

        def write(at, value):
            out[at, pl.ds(c, W)] = value

        multiply(OWN, i, write)

    ready = []
    mates = own_ready = False
    for t in range(NC + LAG[5] + 1):
        for k in (4, 3, 2, 1):
            for i in range(NC):
                if t == max(i - AHEAD, 0) + LAG[k] if k < 3 else t == i + LAG[k]:
                    stage(i, k)
        if t == LEFT_MATE:
            left_mate()
        if t == LEFT_OWN:
            left_own()
            lcopy["s3"].wait_recv()
            own_ready = True
        i = t - LAG[5]
        if 0 <= i < NC:
            for copy in started[i, 4]:
                copy.wait_recv()
            if i < NS:
                if not mates:
                    lcopy["s1"].wait_recv()
                    lcopy["s2"].wait_recv()
                    mates = True
                compute_mate(i)
            ready.append(i)
        if own_ready:
            for _ in range(2):
                if ready:
                    compute_own(ready.pop(0))
    while ready:
        compute_own(ready.pop(0))

    for copies in started.values():
        for copy in copies:
            copy.wait_send()
    for copy in lcopy.values():
        copy.wait_send()
    for copy in outs:
        copy.wait()


LAG = [0, 0, 1, 2, 4, 6]
AHEAD = 4
LEFT_MATE, LEFT_OWN = 4, 8


def shards(left, right):
    flops = 2 * M * N * K
    return pl.pallas_call(
        kernel,
        out_shape=OUT,
        in_specs=[pl.BlockSpec(memory_space=pl.ANY)] * 2,
        out_specs=pl.BlockSpec(memory_space=pltpu.VMEM),
        scratch_shapes=[
            pltpu.VMEM((NC, 4, 2, 4, DEPTH, W), jnp.bfloat16),
            pltpu.VMEM((2, M, K), jnp.bfloat16),
            pltpu.VMEM((NS, M, W), jnp.bfloat16),
            pltpu.SemaphoreType.DMA((NC, 9)),
            pltpu.SemaphoreType.DMA((NC, 9)),
            pltpu.SemaphoreType.DMA((7,)),
            pltpu.SemaphoreType.DMA((7,)),
            pltpu.SemaphoreType.DMA((NS,)),
            pltpu.SemaphoreType.DMA((NS,)),
            pltpu.SemaphoreType.DMA((NC + 1,)),
        ],
        compiler_params=pltpu.CompilerParams(
            collective_id=0, has_side_effects=True, vmem_limit_bytes=50 * 2**20
        ),
        cost_estimate=pl.CostEstimate(flops=flops, bytes_accessed=2 * M * N, transcendentals=0),
    )(left, right)


OUT = jax.ShapeDtypeStruct((M, N), jnp.bfloat16)


def solution(mesh):
    placed = (P("sub", "grp"), P("sub", "grp"))
    return jax.shard_map(
        shards, mesh=mesh, in_specs=placed, out_specs=P("sub", "grp"), check_vma=False
    )
```

time: 281 us -> 128 us (0.46)
  waiting for transfers between devices: 246 us -> 0 us
  Pallas kernels: 0 us -> 115 us
  matrix products: 20.3 us -> 0 us
  between operations: 13.4 us -> 0.01 us
  local copies, waits for them, and re-layouts: 0 us -> 10.7 us
    all_gather x2 -> x0, waiting for transfers between devices: 245 us -> none  [the longest x1 213 us: shards(): right_full = lax.all_gather(right, 'sub', axis=0, tiled=True)]
    pallas_call x0 -> x1, Pallas kernels: none -> 115 us  [shards(): pl.pallas_call(kernel, out_shape=OUT, in_specs=[pl.BlockSpec(memory_space...]
    dot_general x1 -> x0, matrix products: 20.3 us -> none  [shards(): jnp.dot(left_full, right_full, preferred_element_type=jnp.float32)]
    unnamed x0 -> x5, local copies, waits for them, and re-layouts: none -> 10.7 us
  transfers between devices with their start and end apart: 2 -> 0, of which waited for: 2 -> 0; matrix products, arithmetic and copies ran while one was open for 0% -> 0% of each run, Pallas kernels for 0% -> 0%
where the time goes in v1:
time: 128 us; the launch traced here: 126 us
  Pallas kernels  115 us (90%)
  local copies, waits for them, and re-layouts  10.7 us (8%)
    pallas_call x1, Pallas kernels, shards(): pl.pallas_call(kernel, out_shape=OUT, in_specs=[pl.BlockSpec(memory_space...  115 us
    unnamed x5, local copies, waits for them, and re-layouts  10.7 us

profile of v1, /device:TPU:0, one launch (start us, length us, event | category | flops | bytes accessed | tf_op | source)
XLA Modules:
  0.0 126.2 jit_solution(14381537464661729500)
XLA Ops:
  0.0 0.0 copy-start
  0.0 1.1 copy-done
  1.1 0.0 copy-start.1
  1.1 1.1 copy-done.1
  2.1 115.4 %shard_map.28 = bf16[768,6144]{1,0:T(8,128)(2,1)} custom-call(bf16[768,384]{1,0:T(8,128)(2,1)S(1)} %copy-done, bf16[48,6144]{1,0:T(8,128)(2,1)S(1)} %copy-done.1), custom_call_target="tpu_custom_call" | custom-call | flops 14495514624 | bytes 9437184 | tf_op jit(solution)/shard_map/pallas_call | solution.py:190
  117.6 8.6 %copy.4 = bf16[768,6144]{1,0:T(8,128)(2,1)} copy(bf16[768,6144]{1,0:T(8,128)(2,1)} %shard_map.28) | data formatting | bytes 18874368
Async XLA Ops:
  0.0 1.1 copy-start
  1.1 1.1 copy-start.1

commit v2 on v0

v2 whole, which is shorter than its diff:
```python
import jax
import jax.numpy as jnp
from jax import lax
from jax.experimental import pallas as pl
from jax.experimental.pallas import tpu as pltpu
from jax.sharding import PartitionSpec as P

MESH = pl.DeviceIdType.MESH
M, N, K, DEPTH, KL = 768, 6144, 1536, 48, 384
W = 256
NS = 6
ND = N // W - 2 * NS
NC = NS + ND
TILE = 256
OWN, MATE = 0, 1

ORDER = (
    ("z", 1), ("z", 0), ("z", 13), ("z", 2), ("z", 3), ("z", 5), ("z", 10), ("z", 9),
    ("z", 4), (1, 1), (1, 0), (1, 13), ("z", 11), ("L", 0), (1, 2), ("z", 12),
    (1, 3), (1, 10), (1, 5), (2, 1), (2, 0), ("z", 6), (1, 11), (1, 9),
    ("z", 15), ("z", 8), (2, 2), (1, 4), (2, 13), (2, 3), (2, 10), (3, 1),
    (3, 0), (3, 2), (3, 3), ("z", 14), (2, 4), (4, 1), (2, 11), (2, 5),
    ("LM", 0), ("z", 17), (4, 0), (1, 6), ("z", 7), ("z", 16), (4, 2), (1, 14),
    (1, 15), (4, 3), (2, 9), (3, 4), (1, 16), (1, 8), ("m", 1), (1, 12),
    (3, 10), ("m", 2), (2, 14), (2, 6), (2, 16), (1, 17), (1, 7), (3, 13),
    (3, 14), (3, 5), (3, 9), ("LO", 0), (4, 10), (2, 15), (4, 13), (4, 5),
    (2, 17), (2, 7), (2, 8), (2, 12), (3, 16), ("m", 0), (4, 9), ("m", 3),
    (3, 15), (4, 14), (3, 11), (3, 6), (4, 16), ("o", 3), ("o", 1), (4, 4),
    (3, 12), (3, 8), ("m", 5), (3, 7), ("o", 14), ("o", 0), ("o", 13), ("o", 9),
    (4, 6), ("o", 10), (4, 15), ("o", 2), ("m", 4), (3, 17), ("o", 5), ("o", 4),
    ("o", 16), (4, 7), (4, 12), ("o", 15), (4, 8), (4, 11), ("o", 6), (4, 17),
    ("o", 7), ("o", 12), ("o", 8), ("o", 11), ("o", 17),
)


def kernel(left, right, out, held, rows, theirs, zrecv, recv, send, lrecv, lsend, osem, local):
    grp, sub = lax.axis_index("grp"), lax.axis_index("sub")
    zh, core = grp // 2, lax.rem(grp, 2)
    x, zl, y = sub // 8, lax.rem(sub // 4, 2), lax.rem(sub, 4)

    def device(x, y, zh, zl, core):
        return (zh * 2 + core, x * 8 + zl * 4 + y)

    xr, xl, yr, yl = lax.rem(x + 1, 4), lax.rem(x + 3, 4), lax.rem(y + 1, 4), lax.rem(y + 3, 4)
    x_right, x_left = device(xr, y, zh, zl, core), device(xl, y, zh, zl, core)
    y_right, y_left = device(x, yr, zh, zl, core), device(x, yl, zh, zl, core)
    mate = device(x, y, zh, 1 - zl, core)
    cross = device(x, y, 1 - zh, 1 - zl, core)
    sibling = device(x, y, zh, zl, 1 - core)
    around = (x_right, x_left, y_right, y_left, mate, cross, sibling)

    barrier = pltpu.get_barrier_semaphore()
    for other in around:
        pl.semaphore_signal(barrier, inc=1, device_id=other, device_id_type=MESH)

    def column(i, side):
        if i < NS:
            return pl.multiple_of(side * (NS * W) + i * W, 128)
        return (NS + i) * W

    def kcols(g):
        return pl.ds(pl.multiple_of(g * KL, 128), KL)

    def go(src, dst, ssem, rsem, to):
        pltpu.make_async_remote_copy(src, dst, ssem, rsem, device_id=to, device_id_type=MESH).start()

    def wait(like, sem):
        pltpu.make_async_copy(like, like, sem).wait()

    for i in range(NC):
        pltpu.make_async_copy(right.at[:, pl.ds(column(i, zl), W)], held.at[i, x, zl, y], local.at[0]).start()
    mine = pltpu.make_async_copy(left, rows.at[OWN, :, kcols(grp)], local.at[1])
    mine.start()
    with jax.named_scope("barrier"):
        pl.semaphore_wait(barrier, len(around))

    here_k, other_k = kcols(grp), kcols((1 - zh) * 2 + core)
    a_block = rows.at[0, :, pl.ds(0, KL)]
    two_blocks, three_blocks = rows.at[0, :, pl.ds(0, 2 * KL)], rows.at[0, :, pl.ds(0, 3 * KL)]

    def exchange(i):
        src = right.at[:, pl.ds(column(i, 1 - zl), W)]
        go(src, held.at[i, x, zl, y], send.at[0], zrecv.at[i], mate)

    def left_first():
        go(left, rows.at[MATE, :, here_k], lsend.at[0], lrecv.at[0], mate)
        go(left, rows.at[MATE, :, here_k], lsend.at[0], lrecv.at[1], cross)
        go(left, rows.at[OWN, :, here_k], lsend.at[0], lrecv.at[4], sibling)

    def left_mate():
        wait(a_block, lrecv.at[0])
        block = rows.at[MATE, :, here_k]
        go(block, rows.at[OWN, :, here_k], lsend.at[0], lrecv.at[2], cross)
        go(block, block, lsend.at[1], lrecv.at[3], sibling)
        wait(a_block, lrecv.at[1])
        block = rows.at[MATE, :, other_k]
        go(block, block, lsend.at[1], lrecv.at[3], sibling)

    def left_own():
        wait(a_block, lrecv.at[2])
        block = rows.at[OWN, :, other_k]
        go(block, block, lsend.at[1], lrecv.at[4], sibling)
        mine.wait()

    def arrived(i, k):
        like = (None, held.at[i, 0, 0], held.at[i, 0, :, 0], held.at[i, :, 0], held.at[i, 0])[k]
        wait(like, recv.at[i, k - 1])

    def piece(i, along, a, b, z):
        return held.at[i, a, z, b] if along == 0 else held.at[i, b, z, a]

    def stage(i, k):
        first = i % 2
        along = first if k < 3 else 1 - first
        here, lo, hi = ((x, xl, xr), (y, yl, yr))[along]
        fixed = (y, x)[along] if k < 3 else slice(None)
        right_to, left_to = ((x_right, x_left), (y_right, y_left))[along]
        if k == 1:
            wait(held.at[i, 0, 0, 0], zrecv.at[i])
        else:
            arrived(i, k - 1)
        if k in (1, 3):
            up = down = piece(i, along, here, fixed, slice(None))
        else:
            up, down = piece(i, along, lo, fixed, 0), piece(i, along, hi, fixed, 1)
        go(up, up, send.at[k], recv.at[i, k - 1], right_to)
        go(down, down, send.at[k], recv.at[i, k - 1], left_to)

    def multiply(side, i, write):
        block = held.at[i]

        @pl.loop(0, M // TILE)
        def _(t):
            at = pl.ds(pl.multiple_of(t * TILE, TILE), TILE)
            value = jnp.dot(rows[side, at, :], block[...].reshape(K, W), preferred_element_type=jnp.float32)
            write(at, value.astype(jnp.bfloat16))

    def compute_mate(i):
        def write(at, value):
            theirs[i, at, :] = value

        multiply(MATE, i, write)
        go(theirs.at[i], out.at[:, pl.ds(column(i, zl), W)], osem.at[0], osem.at[1], mate)

    def compute_own(i):
        c = column(i, zl)

        def write(at, value):
            out[at, pl.ds(c, W)] = value

        multiply(OWN, i, write)

    met = set()

    def once(what):
        new = what not in met
        met.add(what)
        return new

    def full(i):
        if once(("full", i)):
            with jax.named_scope(f"w4_{i}"):
                arrived(i, 4)

    for op, i in ORDER:
        if op == 1 and once("local"):
            wait(held.at[:, 0, 0, 0], local.at[0])
        if op in ("m", "o"):
            full(i)
        if op == "m" and once("mate"):
            with jax.named_scope("wmate"):
                wait(two_blocks, lrecv.at[3])
        if op == "o" and once("own"):
            with jax.named_scope("wown"):
                wait(two_blocks, lrecv.at[4])
        with jax.named_scope(f"{op}_{i}"):
            if op == "z":
                exchange(i)
            elif op == "L":
                left_first()
            elif op == "LM":
                left_mate()
            elif op == "LO":
                left_own()
            elif op == "m":
                compute_mate(i)
            elif op == "o":
                compute_own(i)
            else:
                stage(i, op)

    with jax.named_scope("sends"):
        for k, like in enumerate(
            (held.at[:, 0, 0, 0], held.at[:, 0, 0], held.at[:, 0, :, 0], held.at[:, :, 0], held.at[:, 0])
        ):
            wait(like, send.at[k])
        wait(rows.at[0], lsend.at[0])
        wait(three_blocks, lsend.at[1])
    with jax.named_scope("outs"):
        wait(theirs, osem.at[0])
        wait(theirs, osem.at[1])


def shards(left, right):
    return pl.pallas_call(
        kernel,
        out_shape=pltpu.VMEM((M, N), jnp.bfloat16),
        in_specs=[pl.BlockSpec(memory_space=pltpu.HBM)] * 2,
        out_specs=pl.BlockSpec(memory_space=pltpu.VMEM),
        scratch_shapes=[
            pltpu.VMEM((NC, 4, 2, 4, DEPTH, W), jnp.bfloat16),
            pltpu.VMEM((2, M, K), jnp.bfloat16),
            pltpu.VMEM((NS, M, W), jnp.bfloat16),
            pltpu.SemaphoreType.DMA((NC,)),
            pltpu.SemaphoreType.DMA((NC, 4)),
            pltpu.SemaphoreType.DMA((5,)),
            pltpu.SemaphoreType.DMA((5,)),
            pltpu.SemaphoreType.DMA((2,)),
            pltpu.SemaphoreType.DMA((2,)),
            pltpu.SemaphoreType.DMA((2,)),
        ],
        compiler_params=pltpu.CompilerParams(
            collective_id=0, has_side_effects=True, vmem_limit_bytes=50 * 2**20
        ),
        cost_estimate=pl.CostEstimate(flops=2 * M * N * K, bytes_accessed=2 * M * N, transcendentals=0),
    )(left, right)


def solution(mesh):
    placed = (P("sub", "grp"), P("sub", "grp"))
    return jax.shard_map(
        shards, mesh=mesh, in_specs=placed, out_specs=P("sub", "grp"), check_vma=False
    )
```

time: 281 us -> 90.8 us (0.32)
  waiting for transfers between devices: 246 us -> 0 us
  Pallas kernels: 0 us -> 87 us
  matrix products: 20.3 us -> 0 us
  between operations: 13.4 us -> 0.01 us
  local copies, waits for them, and re-layouts: 0 us -> 3.74 us
    all_gather x2 -> x0, waiting for transfers between devices: 245 us -> none  [the longest x1 213 us: shards(): right_full = lax.all_gather(right, 'sub', axis=0, tiled=True)]
    pallas_call x0 -> x1, Pallas kernels: none -> 87 us  [shards(): pl.pallas_call(kernel, out_shape=pltpu.VMEM((M, N), jnp.bfloat16), in_spe...]
    dot_general x1 -> x0, matrix products: 20.3 us -> none  [shards(): jnp.dot(left_full, right_full, preferred_element_type=jnp.float32)]
    unnamed x0 -> x1, local copies, waits for them, and re-layouts: none -> 3.74 us
  transfers between devices with their start and end apart: 2 -> 0, of which waited for: 2 -> 0; matrix products, arithmetic and copies ran while one was open for 0% -> 0% of each run, Pallas kernels for 0% -> 0%
where the time goes in v2:
time: 90.8 us; the launch traced here: 90.7 us
  Pallas kernels  87 us (96%)
  local copies, waits for them, and re-layouts  3.74 us (4%)
    pallas_call x1, Pallas kernels, shards(): pl.pallas_call(kernel, out_shape=pltpu.VMEM((M, N), jnp.bfloat16), in_spe...  87 us
    unnamed x1, local copies, waits for them, and re-layouts  3.74 us

profile of v2, /device:TPU:0, one launch (start us, length us, event | category | flops | bytes accessed | tf_op | source)
XLA Modules:
  0.0 90.7 jit_solution(17837786278594274805)
XLA Ops:
  0.0 87.0 %shard_map.28 = bf16[768,6144]{1,0:T(8,128)(2,1)S(1)} custom-call(bf16[768,384]{1,0:T(8,128)(2,1)} %left.1, bf16[48,6144]{1,0:T(8,128)(2,1)} %right.1), custom_call_target="tpu_custom_call" | custom-call | flops 14495514624 | bytes 9437184 | tf_op jit(solution)/shard_map/pallas_call | solution.py:205
  87.0 3.7 %copy.4 = bf16[768,6144]{1,0:T(8,128)(2,1)} copy(bf16[768,6144]{1,0:T(8,128)(2,1)S(1)} %shard_map.28) | data formatting | bytes 18874368

commit v3 on v2

v3 whole, which is shorter than its diff:
```python
import jax
import jax.numpy as jnp
from jax import lax
from jax.experimental import pallas as pl
from jax.experimental.pallas import tpu as pltpu
from jax.sharding import PartitionSpec as P

MESH = pl.DeviceIdType.MESH
M, N, K, DEPTH, KL = 768, 6144, 1536, 48, 384
W = 256
NS = 6
ND = N // W - 2 * NS
NC = NS + ND
LAST = 2
NA = N - LAST * W
TILE = 256
PARTS = 3
OWN, MATE = 0, 1

ORDER = (
    ("z", 4), ("z", 1), ("p", 17), ("p", 10), ("z", 2), ("z", 5), ("p", 13), ("z", 15),
    ("p", 6), ("p", 16), ("p", 4), ("p", 12), ("p", 15), ("p", 11), ("z", 10), ("p", 0),
    ("p", 1), ("z", 0), ("L", 1), (1, 4), ("L", 2), ("p", 14), ("p", 2), (1, 1),
    ("p", 9), (1, 2), (1, 5), ("L", 0), (1, 15), ("p", 5), ("z", 3), (2, 4),
    (2, 1), ("p", 7), (2, 15), ("z", 11), (1, 10), ("z", 8), ("z", 17), ("p", 8),
    (2, 2), ("p", 3), ("z", 9), (1, 0), ("z", 14), ("z", 6), ("z", 16), (2, 5),
    ("z", 13), (3, 4), (3, 1), ("LM", 1), (3, 2), (2, 10), ("LM", 2), (2, 0),
    (4, 4), (4, 1), (3, 15), ("LM", 0), (1, 11), (4, 2), ("LO", 1), (1, 17),
    ("z", 7), (1, 14), (3, 0), (3, 5), ("z", 12), ("m", 1), (2, 11), (1, 12),
    (1, 8), (4, 15), ("m", 4), (1, 7), (2, 17), (1, 16), (4, 0), (1, 6),
    (1, 13), (2, 14), (3, 11), (2, 7), (1, 3), (2, 12), (3, 10), (4, 5),
    (2, 8), ("m", 0), (1, 9), ("m", 2), (2, 16), (2, 3), (4, 10), (2, 13),
    (2, 6), (3, 7), (2, 9), (3, 12), ("LO", 0), ("m", 5), (3, 3), (3, 14),
    ("LO", 2), (4, 7), (4, 11), (3, 6), (4, 3), ("o", 15), (3, 8), ("o", 4),
    (3, 9), ("o", 0), ("o", 1), (4, 14), (4, 6), ("o", 10), (3, 16), (3, 13),
    ("o", 11), (4, 9), (3, 17), ("m", 3), (4, 12), (4, 8), ("o", 2), ("o", 7),
    ("o", 5), ("o", 14), ("o", 3), (4, 13), ("o", 6), (4, 16), ("o", 9), (4, 17),
    ("o", 12), ("o", 8), ("o", 13), ("f", 16), ("f", 17),
)


def gather(left, right, out, own, tail, held, others, theirs, zrecv, recv, send, lrecv, lsend, sibrecv, osem, local):
    grp, sub = lax.axis_index("grp"), lax.axis_index("sub")
    zh, core = grp // 2, lax.rem(grp, 2)
    x, zl, y = sub // 8, lax.rem(sub // 4, 2), lax.rem(sub, 4)

    def device(x, y, zh, zl, core):
        return (zh * 2 + core, x * 8 + zl * 4 + y)

    xr, xl, yr, yl = lax.rem(x + 1, 4), lax.rem(x + 3, 4), lax.rem(y + 1, 4), lax.rem(y + 3, 4)
    x_right, x_left = device(xr, y, zh, zl, core), device(xl, y, zh, zl, core)
    y_right, y_left = device(x, yr, zh, zl, core), device(x, yl, zh, zl, core)
    mate = device(x, y, zh, 1 - zl, core)
    cross = device(x, y, 1 - zh, 1 - zl, core)
    sibling = device(x, y, zh, zl, 1 - core)
    around = (x_right, x_left, y_right, y_left, mate, cross, sibling)

    rows = (own, others)

    def chunk(i):
        return held.at[i] if i < NC - LAST else tail.at[i - (NC - LAST)]

    barrier = pltpu.get_barrier_semaphore()
    for other in around:
        pl.semaphore_signal(barrier, inc=1, device_id=other, device_id_type=MESH)

    def column(i, side):
        if i < NS:
            return pl.multiple_of(side * (NS * W) + i * W, 128)
        return (NS + i) * W

    def kcols(g):
        return pl.ds(pl.multiple_of(g * KL, 128), KL)

    def go(src, dst, ssem, rsem, to):
        pltpu.make_async_remote_copy(src, dst, ssem, rsem, device_id=to, device_id_type=MESH).start()

    def wait(like, sem):
        pltpu.make_async_copy(like, like, sem).wait()

    for i in range(NC):
        pltpu.make_async_copy(right.at[:, pl.ds(column(i, zl), W)], chunk(i).at[x, zl, y], local.at[0]).start()
    mine = pltpu.make_async_copy(left, own.at[:, kcols(grp)], local.at[1])
    mine.start()
    with jax.named_scope("barrier"):
        pl.semaphore_wait(barrier, len(around))

    here_k, other_k = kcols(grp), kcols((1 - zh) * 2 + core)
    some = NC // 2
    a_part = own.at[pl.ds(0, M // PARTS), pl.ds(0, KL)]
    two_blocks, three_blocks = own.at[:, pl.ds(0, 2 * KL)], own.at[:, pl.ds(0, 3 * KL)]

    def exchange(i):
        src = right.at[:, pl.ds(column(i, 1 - zl), W)]
        go(src, chunk(i).at[x, zl, y], send.at[0], zrecv.at[i], mate)

    def part(j):
        return pl.ds(j * (M // PARTS), M // PARTS)

    def left_first(j):
        go(left.at[part(j)], others.at[part(j), here_k], lsend.at[0], lrecv.at[0, j], mate)
        go(left.at[part(j)], others.at[part(j), here_k], lsend.at[0], lrecv.at[1, j], cross)
        go(left.at[part(j)], own.at[part(j), here_k], lsend.at[0], sibrecv.at[1], sibling)

    def left_mate(j):
        wait(a_part, lrecv.at[0, j])
        block = others.at[part(j), here_k]
        go(block, own.at[part(j), here_k], lsend.at[0], lrecv.at[2, j], cross)
        go(block, block, lsend.at[1], sibrecv.at[0], sibling)
        wait(a_part, lrecv.at[1, j])
        block = others.at[part(j), other_k]
        go(block, block, lsend.at[1], sibrecv.at[0], sibling)

    def left_own(j):
        wait(a_part, lrecv.at[2, j])
        block = own.at[part(j), other_k]
        go(block, block, lsend.at[1], sibrecv.at[1], sibling)

    def arrived(i, k):
        like = (None, held.at[0, 0, 0], held.at[0, 0, :, 0], held.at[0, 0], held.at[0, :, 0])[k]
        wait(like, recv.at[i, k - 1])

    def piece(i, along, a, b, z):
        return chunk(i).at[a, z, b] if along == 0 else chunk(i).at[b, z, a]

    def both(i, k, up, down, to):
        go(up, up, send.at[k], recv.at[i, k - 1], to[0])
        go(down, down, send.at[k], recv.at[i, k - 1], to[1])

    def stage(i, k):
        first = i % 2
        along = first if k < 3 else 1 - first
        here, lo, hi = ((x, xl, xr), (y, yl, yr))[along]
        fixed = (y, x)[along] if k < 3 else slice(None)
        to = ((x_right, x_left), (y_right, y_left))[along]
        if k == 0:
            src, dst = right.at[:, pl.ds(column(i, zl), W)], chunk(i).at[x, zl, y]
            go(src, dst, send.at[1], recv.at[i, 0], to[0])
            go(src, dst, send.at[1], recv.at[i, 0], to[1])
        elif k == 1:
            wait(held.at[0, 0, 0, 0], zrecv.at[i])
            block = chunk(i).at[x, 1 - zl, y]
            both(i, 1, block, block, to)
        else:
            arrived(i, k - 1)
            if k == 3:
                low, high = piece(i, along, here, fixed, 0), piece(i, along, here, fixed, 1)
                both(i, 3, low, high, to)
                go(high, high, send.at[3], recv.at[i, 3], to[0])
                go(low, low, send.at[3], recv.at[i, 3], to[1])
            else:
                both(i, k, piece(i, along, lo, fixed, 0), piece(i, along, hi, fixed, 1), to)

    def multiply(side, i, write):
        block = chunk(i)

        @pl.loop(0, M // TILE)
        def _(t):
            at = pl.ds(pl.multiple_of(t * TILE, TILE), TILE)
            value = jnp.dot(rows[side][at, :], block[...].reshape(K, W), preferred_element_type=jnp.float32)
            write(at, value.astype(jnp.bfloat16))

    def compute_mate(i):
        def write(at, value):
            theirs[i, at, :] = value

        multiply(MATE, i, write)
        go(theirs.at[i], out.at[:, pl.ds(column(i, zl), W)], osem.at[0], osem.at[1], mate)

    def compute_own(i):
        c = column(i, zl)

        def write(at, value):
            out[at, pl.ds(c, W)] = value

        multiply(OWN, i, write)

    met = set()

    def once(what):
        new = what not in met
        met.add(what)
        return new

    def full(i):
        if once(("full", i)):
            with jax.named_scope(f"w4_{i}"):
                arrived(i, 4)

    for op, i in ORDER:
        if op == 3 and once("local"):
            wait(held.at[pl.ds(0, some), 0, :, 0], local.at[0])
        if op in ("m", "o", "f"):
            full(i)
        if op == "m" and once("mate"):
            with jax.named_scope("wmate"):
                wait(two_blocks, sibrecv.at[0])
        if op == "o" and once("own"):
            with jax.named_scope("wown"):
                wait(two_blocks, sibrecv.at[1])
                mine.wait()
        with jax.named_scope(f"{op}_{i}"):
            if op == "z":
                exchange(i)
            elif op == "p":
                stage(i, 0)
            elif op == "L":
                left_first(i)
            elif op == "LM":
                left_mate(i)
            elif op == "LO":
                left_own(i)
            elif op == "m":
                compute_mate(i)
            elif op == "o":
                compute_own(i)
            elif op != "f":
                stage(i, op)

    with jax.named_scope("sends"):
        for k, like in enumerate((
            held.at[pl.ds(0, some), 0, :, 0],
            held.at[pl.ds(0, some), 0],
            held.at[pl.ds(0, some), 0, 0],
            held.at[pl.ds(0, some)],
            held.at[pl.ds(0, some), :, 0],
        )):
            wait(like, send.at[k])
        wait(own, lsend.at[0])
        wait(three_blocks, lsend.at[1])
    with jax.named_scope("outs"):
        wait(theirs, osem.at[0])
        wait(theirs, osem.at[1])


def finish(done, own, tail, out, last, sems):
    copies = []
    for b in range(BLOCKS):
        at = pl.ds(b * (M // BLOCKS), M // BLOCKS)
        copies.append(pltpu.make_async_copy(done.at[at], out.at[at, pl.ds(0, NA)], sems.at[b]))
        copies[-1].start()
    for j in range(LAST):

        @pl.loop(0, M // TILE)
        def _(t):
            at = pl.ds(pl.multiple_of(t * TILE, TILE), TILE)
            value = jnp.dot(own[at, :], tail[j].reshape(K, W), preferred_element_type=jnp.float32)
            last[j, at, :] = value.astype(jnp.bfloat16)

        copies.append(pltpu.make_async_copy(last.at[j], out.at[:, pl.ds(NA + j * W, W)], sems.at[BLOCKS + j]))
        copies[-1].start()
    for copy in copies:
        copy.wait()


BLOCKS = 4


def shards(left, right):
    chunks = (4, 2, 4, DEPTH, W)
    done, own, tail = pl.pallas_call(
        gather,
        out_shape=(
            pltpu.VMEM((M, NA), jnp.bfloat16),
            pltpu.VMEM((M, K), jnp.bfloat16),
            pltpu.VMEM((LAST,) + chunks, jnp.bfloat16),
        ),
        in_specs=[pl.BlockSpec(memory_space=pltpu.HBM)] * 2,
        out_specs=(pl.BlockSpec(memory_space=pltpu.VMEM),) * 3,
        scratch_shapes=[
            pltpu.VMEM((NC - LAST,) + chunks, jnp.bfloat16),
            pltpu.VMEM((M, K), jnp.bfloat16),
            pltpu.VMEM((NS, M, W), jnp.bfloat16),
            pltpu.SemaphoreType.DMA((NC,)),
            pltpu.SemaphoreType.DMA((NC, 4)),
            pltpu.SemaphoreType.DMA((5,)),
            pltpu.SemaphoreType.DMA((3, PARTS)),
            pltpu.SemaphoreType.DMA((2,)),
            pltpu.SemaphoreType.DMA((2,)),
            pltpu.SemaphoreType.DMA((2,)),
            pltpu.SemaphoreType.DMA((2,)),
        ],
        compiler_params=pltpu.CompilerParams(
            collective_id=0, has_side_effects=True, vmem_limit_bytes=GRANT
        ),
        cost_estimate=pl.CostEstimate(flops=2 * M * NA * K, bytes_accessed=2 * M * N, transcendentals=0),
    )(left, right)
    return pl.pallas_call(
        finish,
        out_shape=jax.ShapeDtypeStruct((M, N), jnp.bfloat16),
        in_specs=[pl.BlockSpec(memory_space=pltpu.VMEM)] * 3,
        out_specs=pl.BlockSpec(memory_space=pltpu.HBM),
        scratch_shapes=[pltpu.VMEM((LAST, M, W), jnp.bfloat16), pltpu.SemaphoreType.DMA((BLOCKS + LAST,))],
        compiler_params=pltpu.CompilerParams(vmem_limit_bytes=16 * 2**20),
        cost_estimate=pl.CostEstimate(flops=2 * M * LAST * W * K, bytes_accessed=4 * M * N, transcendentals=0),
    )(done, own, tail)


GRANT = 48 * 2**20


def solution(mesh):
    placed = (P("sub", "grp"), P("sub", "grp"))
    return jax.shard_map(
        shards, mesh=mesh, in_specs=placed, out_specs=P("sub", "grp"), check_vma=False
    )
```

time: 90.8 us -> 86.9 us (0.957)
  local copies, waits for them, and re-layouts: 3.74 us -> 0 us
    unnamed x1 -> x0, local copies, waits for them, and re-layouts: 3.74 us -> none
    pallas_call x1 -> x2, Pallas kernels: 87 us -> 86.7 us  [the longest x1 83.1 us: shards(): pl.pallas_call(gather, out_shape=(pltpu.VMEM((M, NA), jnp.bfloat16), pltp...]
where the time goes in v3:
time: 86.9 us; the launch traced here: 86.8 us
  Pallas kernels  86.7 us (100%)
    pallas_call x1, Pallas kernels, shards(): pl.pallas_call(gather, out_shape=(pltpu.VMEM((M, NA), jnp.bfloat16), pltp...  83.1 us
    pallas_call x1, Pallas kernels, shards(): pl.pallas_call(finish, out_shape=jax.ShapeDtypeStruct((M, N), jnp.bfloat1...  3.64 us

profile of v3, /device:TPU:0, one launch (start us, length us, event | category | flops | bytes accessed | tf_op | source)
XLA Modules:
  0.0 86.8 jit_solution(1080978204376860745)
XLA Ops:
  0.0 83.1 %shard_map.28 = (bf16[768,5632]{1,0:T(8,128)(2,1)S(1)}, bf16[768,1536]{1,0:T(8,128)(2,1)S(1)}, bf16[2,4,2,4,48,256]{5,4,3,2,1,0:T(8,128)(2,1)S(1)}) custom-call(bf16[768,384]{1,0:T(8,128)(2,1)} %left.1, bf16[48,6144]{1,0:T(8,128)(2,1)} %right.1), custom_call_target="tpu_custom_call" | custom-call | flops 13287555072 | bytes 9437184 | tf_op jit(solution)/shard_map/pallas_call | solution.py:261
  83.1 3.6 %shard_map.29 = bf16[768,6144]{1,0:T(8,128)(2,1)} custom-call(bf16[768,5632]{1,0:T(8,128)(2,1)S(1)} %get-tuple-element.8.done, bf16[768,1536]{1,0:T(8,128)(2,1)S(1)} %get-tuple-element.9.own, bf16[2,4,2,4,48,256]{5,4,3,2,1,0:T(8,128)(2,1)S(1)} %get-tuple-element.10.tail), custom_call_target="tpu_custom_call" | custom-call | flops 1207959552 | bytes 18874368 | tf_op jit(solution)/shard_map/pallas_call | solution.py:288

commit v4 on v3

--- a/solution.py
+++ b/solution.py
@@ -18,24 +18,24 @@
 OWN, MATE = 0, 1
 
 ORDER = (
-    ("z", 4), ("z", 1), ("p", 17), ("p", 10), ("z", 2), ("z", 5), ("p", 13), ("z", 15),
-    ("p", 6), ("p", 16), ("p", 4), ("p", 12), ("p", 15), ("p", 11), ("z", 10), ("p", 0),
-    ("p", 1), ("z", 0), ("L", 1), (1, 4), ("L", 2), ("p", 14), ("p", 2), (1, 1),
-    ("p", 9), (1, 2), (1, 5), ("L", 0), (1, 15), ("p", 5), ("z", 3), (2, 4),
-    (2, 1), ("p", 7), (2, 15), ("z", 11), (1, 10), ("z", 8), ("z", 17), ("p", 8),
-    (2, 2), ("p", 3), ("z", 9), (1, 0), ("z", 14), ("z", 6), ("z", 16), (2, 5),
-    ("z", 13), (3, 4), (3, 1), ("LM", 1), (3, 2), (2, 10), ("LM", 2), (2, 0),
-    (4, 4), (4, 1), (3, 15), ("LM", 0), (1, 11), (4, 2), ("LO", 1), (1, 17),
-    ("z", 7), (1, 14), (3, 0), (3, 5), ("z", 12), ("m", 1), (2, 11), (1, 12),
-    (1, 8), (4, 15), ("m", 4), (1, 7), (2, 17), (1, 16), (4, 0), (1, 6),
-    (1, 13), (2, 14), (3, 11), (2, 7), (1, 3), (2, 12), (3, 10), (4, 5),
-    (2, 8), ("m", 0), (1, 9), ("m", 2), (2, 16), (2, 3), (4, 10), (2, 13),
-    (2, 6), (3, 7), (2, 9), (3, 12), ("LO", 0), ("m", 5), (3, 3), (3, 14),
-    ("LO", 2), (4, 7), (4, 11), (3, 6), (4, 3), ("o", 15), (3, 8), ("o", 4),
-    (3, 9), ("o", 0), ("o", 1), (4, 14), (4, 6), ("o", 10), (3, 16), (3, 13),
-    ("o", 11), (4, 9), (3, 17), ("m", 3), (4, 12), (4, 8), ("o", 2), ("o", 7),
-    ("o", 5), ("o", 14), ("o", 3), (4, 13), ("o", 6), (4, 16), ("o", 9), (4, 17),
-    ("o", 12), ("o", 8), ("o", 13), ("f", 16), ("f", 17),
+    ("z", 4), ("z", 1), ("z", 9), ("p", 4), ("p", 9), ("z", 12), ("z", 5), ("p", 14),
+    ("z", 3), ("p", 15), ("z", 16), ("p", 13), ("z", 15), ("p", 11), ("p", 2), ("z", 14),
+    ("p", 1), ("z", 2), ("z", 0), ("L", 1), ("p", 10), ("L", 0), ("L", 2), (1, 4),
+    (1, 1), ("p", 0), (1, 9), (1, 12), ("z", 6), ("p", 12), (1, 5), ("p", 5),
+    ("p", 16), ("z", 13), ("p", 7), (1, 16), (1, 15), (2, 4), ("p", 8), ("z", 11),
+    (1, 14), ("p", 6), (2, 1), ("z", 10), ("p", 17), (1, 0), ("p", 3), (1, 3),
+    (2, 5), (1, 2), (2, 12), (2, 9), ("z", 7), (2, 16), (3, 4), (3, 1),
+    (2, 15), (2, 3), (2, 2), (2, 14), ("LM", 1), (4, 4), (3, 5), (4, 1),
+    (3, 12), ("LM", 0), ("z", 17), ("LM", 2), ("z", 8), (3, 2), (3, 3), (2, 0),
+    (1, 11), (1, 6), (3, 14), (3, 9), ("m", 4), (4, 5), (4, 3), (1, 10),
+    (1, 7), (4, 12), (1, 8), ("m", 1), (3, 0), ("LO", 2), ("LO", 0), (3, 15),
+    ("LO", 1), (1, 13), (1, 17), (2, 7), (2, 11), (4, 2), ("m", 3), (4, 14),
+    (2, 8), (2, 6), (4, 0), (4, 9), (3, 7), (3, 6), (2, 13), (3, 11),
+    (2, 17), ("m", 2), ("m", 0), ("m", 5), (3, 8), (4, 15), (2, 10), ("o", 2),
+    (4, 6), ("o", 9), ("o", 0), (3, 13), ("o", 5), (4, 11), ("o", 3), ("o", 14),
+    (4, 7), (4, 8), (3, 10), (3, 16), (3, 17), ("o", 12), ("o", 1), (4, 13),
+    ("o", 4), (4, 10), ("o", 11), ("o", 8), ("o", 15), ("o", 6), (4, 17), (4, 16),
+    ("o", 7), ("o", 10), ("o", 13), ("f", 17), ("f", 16),
 )
 
 
@@ -154,7 +154,7 @@
     def multiply(side, i, write):
         block = chunk(i)
 
-        @pl.loop(0, M // TILE)
+        @pl.loop(0, M // TILE, unroll=M // TILE)
         def _(t):
             at = pl.ds(pl.multiple_of(t * TILE, TILE), TILE)
             value = jnp.dot(rows[side][at, :], block[...].reshape(K, W), preferred_element_type=jnp.float32)
@@ -241,7 +241,7 @@
         copies[-1].start()
     for j in range(LAST):
 
-        @pl.loop(0, M // TILE)
+        @pl.loop(0, M // TILE, unroll=M // TILE)
         def _(t):
             at = pl.ds(pl.multiple_of(t * TILE, TILE), TILE)
             value = jnp.dot(own[at, :], tail[j].reshape(K, W), preferred_element_type=jnp.float32)

time: 86.9 us -> 85.4 us (0.983)
  Pallas kernels: 86.7 us -> 85.1 us
    pallas_call x1, Pallas kernels: 83.1 us -> 81.5 us  [shards(): pl.pallas_call(gather, out_shape=(pltpu.VMEM((M, NA), jnp.bfloat16), pltp...]
where the time goes in v4:
time: 85.4 us; the launch traced here: 85.3 us
  Pallas kernels  85.1 us (100%)
    pallas_call x1, Pallas kernels, shards(): pl.pallas_call(gather, out_shape=(pltpu.VMEM((M, NA), jnp.bfloat16), pltp...  81.5 us
    pallas_call x1, Pallas kernels, shards(): pl.pallas_call(finish, out_shape=jax.ShapeDtypeStruct((M, N), jnp.bfloat1...  3.66 us

profile of v4, /device:TPU:0, one launch (start us, length us, event | category | flops | bytes accessed | tf_op | source)
XLA Modules:
  0.0 85.3 jit_solution(716709650231518356)
XLA Ops:
  0.0 81.5 %shard_map.28 = (bf16[768,5632]{1,0:T(8,128)(2,1)S(1)}, bf16[768,1536]{1,0:T(8,128)(2,1)S(1)}, bf16[2,4,2,4,48,256]{5,4,3,2,1,0:T(8,128)(2,1)S(1)}) custom-call(bf16[768,384]{1,0:T(8,128)(2,1)} %left.1, bf16[48,6144]{1,0:T(8,128)(2,1)} %right.1), custom_call_target="tpu_custom_call" | custom-call | flops 13287555072 | bytes 9437184 | tf_op jit(solution)/shard_map/pallas_call | solution.py:261
  81.5 3.7 %shard_map.29 = bf16[768,6144]{1,0:T(8,128)(2,1)} custom-call(bf16[768,5632]{1,0:T(8,128)(2,1)S(1)} %get-tuple-element.8.done, bf16[768,1536]{1,0:T(8,128)(2,1)S(1)} %get-tuple-element.9.own, bf16[2,4,2,4,48,256]{5,4,3,2,1,0:T(8,128)(2,1)S(1)} %get-tuple-element.10.tail), custom_call_target="tpu_custom_call" | custom-call | flops 1207959552 | bytes 18874368 | tf_op jit(solution)/shard_map/pallas_call | solution.py:288

commit v5 on v4

--- a/solution.py
+++ b/solution.py
@@ -16,6 +16,11 @@
 TILE = 256
 PARTS = 3
 OWN, MATE = 0, 1
+
+NAMES = {
+    "z": "exchange_z", "p": "send_own_rows", 1: "send_pair_rows", 2: "send_first_axis", 3: "send_blocks", 4: "send_second_axis",
+    "m": "product_mate", "o": "product_own", "f": "chunk_whole", "L": "left_first", "LM": "left_mate", "LO": "left_own",
+}
 
 ORDER = (
     ("z", 4), ("z", 1), ("z", 9), ("p", 4), ("p", 9), ("z", 12), ("z", 5), ("p", 14),
@@ -184,7 +189,7 @@
 
     def full(i):
         if once(("full", i)):
-            with jax.named_scope(f"w4_{i}"):
+            with jax.named_scope("wait_chunk"):
                 arrived(i, 4)
 
     for op, i in ORDER:
@@ -193,13 +198,13 @@
         if op in ("m", "o", "f"):
             full(i)
         if op == "m" and once("mate"):
-            with jax.named_scope("wmate"):
+            with jax.named_scope("wait_left_mate"):
                 wait(two_blocks, sibrecv.at[0])
         if op == "o" and once("own"):
-            with jax.named_scope("wown"):
+            with jax.named_scope("wait_left_own"):
                 wait(two_blocks, sibrecv.at[1])
                 mine.wait()
-        with jax.named_scope(f"{op}_{i}"):
+        with jax.named_scope(NAMES[op]):
             if op == "z":
                 exchange(i)
             elif op == "p":
@@ -217,7 +222,7 @@
             elif op != "f":
                 stage(i, op)
 
-    with jax.named_scope("sends"):
+    with jax.named_scope("wait_sends"):
         for k, like in enumerate((
             held.at[pl.ds(0, some), 0, :, 0],
             held.at[pl.ds(0, some), 0],
@@ -228,7 +233,7 @@
             wait(like, send.at[k])
         wait(own, lsend.at[0])
         wait(three_blocks, lsend.at[1])
-    with jax.named_scope("outs"):
+    with jax.named_scope("wait_products"):
         wait(theirs, osem.at[0])
         wait(theirs, osem.at[1])
 

time: 85.4 us -> 85.4 us (level)
  no operation moved by 1% of the time
where the time goes in v5:
time: 85.4 us; the launch traced here: 85.3 us
  Pallas kernels  85.1 us (100%)
    pallas_call x1, Pallas kernels, shards(): pl.pallas_call(gather, out_shape=(pltpu.VMEM((M, NA), jnp.bfloat16), pltp...  81.5 us
    pallas_call x1, Pallas kernels, shards(): pl.pallas_call(finish, out_shape=jax.ShapeDtypeStruct((M, N), jnp.bfloat1...  3.66 us

profile of v5, /device:TPU:0, one launch (start us, length us, event | category | flops | bytes accessed | tf_op | source)
XLA Modules:
  0.0 85.3 jit_solution(716709650231518356)
XLA Ops:
  0.0 81.5 %shard_map.28 = (bf16[768,5632]{1,0:T(8,128)(2,1)S(1)}, bf16[768,1536]{1,0:T(8,128)(2,1)S(1)}, bf16[2,4,2,4,48,256]{5,4,3,2,1,0:T(8,128)(2,1)S(1)}) custom-call(bf16[768,384]{1,0:T(8,128)(2,1)} %left.1, bf16[48,6144]{1,0:T(8,128)(2,1)} %right.1), custom_call_target="tpu_custom_call" | custom-call | flops 13287555072 | bytes 9437184 | tf_op jit(solution)/shard_map/pallas_call | solution.py:266
  81.5 3.7 %shard_map.29 = bf16[768,6144]{1,0:T(8,128)(2,1)} custom-call(bf16[768,5632]{1,0:T(8,128)(2,1)S(1)} %get-tuple-element.8.done, bf16[768,1536]{1,0:T(8,128)(2,1)S(1)} %get-tuple-element.9.own, bf16[2,4,2,4,48,256]{5,4,3,2,1,0:T(8,128)(2,1)S(1)} %get-tuple-element.10.tail), custom_call_target="tpu_custom_call" | custom-call | flops 1207959552 | bytes 18874368 | tf_op jit(solution)/shard_map/pallas_call | solution.py:293
